TPU v7x, 256 devices: a whole 4x4x8 slice. The times are simulated.
256 devices in a mesh: row: 16 (over z_lo, x), col: 16 (over z_hi, y, core).
Axes of the slice: x: 4, y: 4, z: 8 (z_hi: 2, z_lo: 4; z = z_hi * 4 + z_lo), core: 2. Of those that a mesh axis runs over, the one named last changes fastest.
Arguments:
- leaf_multipoles: float32 [121, 64, 64, 48], P(None, 'row', 'col'), may hold values from -6 to 6
- occupancy: int32 [64, 64, 48], P('row', 'col'), may hold values 0 or 1
- m2m_ops: bfloat16 [2, 2, 2, 121, 121], replicated, may hold values from -0.1875 to 0.1875
- m2l_ops: bfloat16 [7, 7, 7, 121, 121], replicated, may hold values from -0.078125 to 0.078125
- l2l_ops: bfloat16 [2, 2, 2, 121, 121], replicated, may hold values from -0.375 to 0.375
Outputs:
- local_expansions: float32 [121, 64, 64, 48], P(None, 'row', 'col')
All inputs are finite; a program needn't handle non-finite values. No bound on the sum of `occupancy` on one device may be relied on, other than what follows from the above.
Results may differ from a plain program's by a relative error of at most 0.006.
Values may be sent and summed in bfloat16 or wider, within the bound.
A program may use at most 128 MiB of HBM per device.

v0:
```python
import functools

import jax
import jax.numpy as jnp
from jax import lax
from jax.experimental import pallas as pl
from jax.experimental.pallas import tpu as pltpu
from jax.sharding import PartitionSpec as P

MESH = pl.DeviceIdType.MESH
C = 121
F32 = jnp.float32
BF16 = jnp.bfloat16
AROUND = [(dr, dc) for dr in (-1, 0, 1) for dc in (-1, 0, 1) if (dr, dc) != (0, 0)]
MATES = [(0, 1), (1, 0), (1, 1)]


def dot(x, w):
    return jnp.dot(x, w, preferred_element_type=F32)


def swap(v):
    return 2 * (v % 2) + v // 2


def kernel(
    leaf, occ, wm, wl, ops_hbm,
    out,
    ops, opt, s6, w6, n5, w5, w4, n4, t3, m3, n3, n2, nat, col, t6, ts, f6, fs, ls,
    ops_sem, s6_send, s6_recv, s5_send, s5_recv, a_send, a_recv, b_send, b_recv,
    c_send, c_recv, d_send, d_recv,
):
    r, c = lax.axis_index("row"), lax.axis_index("col")
    nr, nc = lax.axis_size("row"), lax.axis_size("col")

    ops_copies = [
        pltpu.make_async_copy(ops_hbm.at[dx], ops.at[dx], ops_sem.at[dx]) for dx in range(7)
    ]
    for copy in ops_copies:
        copy.start()

    def inside(rr, cc):
        return (rr >= 0) & (rr < nr) & (cc >= 0) & (cc < nc)

    def partner(n):
        return 4 * (n // 4) + swap(r % 4), 4 * (n % 4) + swap(c % 4)

    barrier = pltpu.get_barrier_semaphore()
    greeted = jnp.int32(0)
    for scale in (1, 2):
        for dr, dc in AROUND:
            rr, cc = r + scale * dr, c + scale * dc
            there = inside(rr, cc)

            @pl.when(there)
            def _():
                pl.semaphore_signal(
                    barrier, inc=1, device_id={"row": rr, "col": cc}, device_id_type=MESH
                )

            greeted = greeted + there.astype(jnp.int32)
    for n in range(16):
        rr, cc = partner(n)
        other = (rr != r) | (cc != c)

        @pl.when(other)
        def _():
            pl.semaphore_signal(
                barrier, inc=1, device_id={"row": rr, "col": cc}, device_id_type=MESH
            )

        greeted = greeted + other.astype(jnp.int32)

    s6[...] = jnp.zeros_like(s6)
    occ_t = jnp.transpose(
        jnp.concatenate([occ[x].astype(F32) for x in range(4)], axis=0)
    )
    for x in range(4):
        for y in range(4):
            here = 4 * x + y
            s6[x, y, :, 0:C] = leaf[x, y] * occ_t[:, here : here + 1]
    for x in range(2):
        for y in range(4):
            for a in range(2):
                w6[1 + x, 2 + y, :, a * 128 : (a + 1) * 128] = s6[2 * x + a, y].astype(BF16)

    total = jnp.zeros((96, 128), F32)
    for b in range(2):
        for cz in range(2):
            rows = []
            for x in range(2):
                for y in range(2):
                    rows.append(
                        jnp.concatenate(
                            [s6[2 * x + a, 2 * y + b, pl.ds(cz, 24, stride=2), :] for a in range(2)],
                            axis=1,
                        )
                    )
            total = total + dot(jnp.concatenate(rows, axis=0).astype(BF16), wm[2 * b + cz])
    n5[:, 48:64, :] = jnp.zeros((2, 16, 128), F32)
    for x in range(2):
        n5[x, 0:48, :] = total[48 * x : 48 * x + 48]
        w5[1, 1, :, 128 * x : 128 * x + 128] = total[48 * x : 48 * x + 48].astype(BF16)

    total = jnp.zeros((16, 128), F32)
    for b in range(2):
        for cz in range(2):
            rows = jnp.concatenate(
                [n5[a, pl.ds(24 * b + cz, 16, stride=2), :] for a in range(2)], axis=1
            )
            total = total + dot(rows.astype(BF16), wm[2 * b + cz])
    depth = lax.broadcasted_iota(jnp.int32, (16, 128), 0)
    w4[1, 1, r % 2, c % 2] = jnp.where(depth < 12, total, 0.0).astype(BF16)

    @pl.when(r == 0)
    def _():
        w6[0] = jnp.zeros_like(w6[0])
        w5[0] = jnp.zeros_like(w5[0])

    @pl.when(r == nr - 1)
    def _():
        w6[3] = jnp.zeros_like(w6[3])
        w5[2] = jnp.zeros_like(w5[2])

    @pl.when(c == 0)
    def _():
        w6[:, 0:2] = jnp.zeros_like(w6[:, 0:2])
        w5[:, 0] = jnp.zeros_like(w5[:, 0])

    @pl.when(c == nc - 1)
    def _():
        w6[:, 6:8] = jnp.zeros_like(w6[:, 6:8])
        w5[:, 2] = jnp.zeros_like(w5[:, 2])

    @pl.when(r // 2 == 0)
    def _():
        w4[0] = jnp.zeros_like(w4[0])

    @pl.when(r // 2 == nr // 2 - 1)
    def _():
        w4[2] = jnp.zeros_like(w4[2])

    @pl.when(c // 2 == 0)
    def _():
        w4[:, 0] = jnp.zeros_like(w4[:, 0])

    @pl.when(c // 2 == nc // 2 - 1)
    def _():
        w4[:, 2] = jnp.zeros_like(w4[:, 2])

    pl.semaphore_wait(barrier, greeted)

    def remote(src, dst, send, recv, rr, cc):
        return pltpu.make_async_remote_copy(
            src_ref=src,
            dst_ref=dst,
            send_sem=send,
            recv_sem=recv,
            device_id={"row": rr, "col": cc},
            device_id_type=MESH,
        )

    def mate_copy(n):
        dr, dc = MATES[n]
        tile = w4.at[1, 1, r % 2, c % 2]
        return remote(
            tile, tile, a_send.at[n], a_recv.at[n], r + dr * (1 - 2 * (r % 2)), c + dc * (1 - 2 * (c % 2))
        )

    def mate_landing(n):
        dr, dc = MATES[n]
        tile = w4.at[1, 1, (r + dr) % 2, (c + dc) % 2]
        return remote(tile, tile, a_send.at[n], a_recv.at[n], r, c)

    def span(d, own, low, high, width):
        if d == 0:
            return pl.ds(own, 2 * width), pl.ds(own, 2 * width)
        if d < 0:
            return pl.ds(own, width), pl.ds(high, width)
        return pl.ds(own + width, width), pl.ds(low, width)

    def rim_copy(n):
        dr, dc = AROUND[n]
        sx, tx = span(dr, 1, 0, 3, 1)
        sy, ty = span(dc, 2, 0, 6, 2)
        return remote(
            w6.at[sx, sy], w6.at[tx, ty], s6_send.at[n], s6_recv.at[n], r + dr, c + dc
        )

    def five_copy(n):
        dr, dc = AROUND[n]
        return remote(
            w5.at[1, 1], w5.at[1 - dr, 1 - dc], s5_send.at[n], s5_recv.at[n], r + dr, c + dc
        )

    def four_copy(n):
        dr, dc = AROUND[n]
        return remote(
            w4.at[1, 1], w4.at[1 - dr, 1 - dc], b_send.at[n], b_recv.at[n], r + 2 * dr, c + 2 * dc
        )

    def sends_to(n, scale):
        dr, dc = AROUND[n]
        return inside(r + scale * dr, c + scale * dc)

    def gets_from(n, scale):
        dr, dc = AROUND[n]
        return inside(r - scale * dr, c - scale * dc)

    def each(make, scale, wanted, act):
        for n in range(8):

            @pl.when(wanted(n, scale))
            def _():
                act(make(n))

    for n in range(3):
        mate_copy(n).start()
    each(five_copy, 1, sends_to, lambda copy: copy.start())
    each(rim_copy, 1, sends_to, lambda copy: copy.start())

    opt_pad = jnp.zeros((7, 128), BF16)
    opt_side = jnp.zeros((128, 7), BF16)

    def turn(dx):
        ops_copies[dx].wait()

        def one(n, _):
            dy, dz = n // 7, n % 7
            block = jnp.concatenate(
                [jnp.concatenate([ops[dx, dy, dz], opt_pad[:, 0:C]], axis=0), opt_side], axis=1
            )
            opt[dx, dy, dz] = jnp.transpose(block)
            return 0

        lax.fori_loop(0, 49, one, 0)
        if 2 <= dx <= 4:
            for dy in range(2, 5):
                for dz in range(2, 5):
                    opt[dx, dy, dz] = jnp.zeros((128, 128), BF16)

    for dx in (0, 1):
        turn(dx)

    for n in range(3):
        mate_landing(n).wait_recv()
    for b in range(2):
        for a in range(2):
            n4[b, a] = w4[1, 1, a, b].astype(F32)
    total = jnp.zeros((16, 128), F32)
    for b in range(2):
        for cz in range(2):
            rows = jnp.concatenate(
                [
                    jnp.concatenate([n4[b, a, pl.ds(cz, 8, stride=2), :] for a in range(2)], axis=1),
                    jnp.zeros((8, 256), F32),
                ],
                axis=0,
            )
            total = total + dot(rows.astype(BF16), wm[2 * b + cz])
    t3[...] = jnp.where(depth < 6, total, 0.0).astype(BF16)

    def three_copy(n):
        rr, cc = partner(n)
        return remote(
            t3,
            m3.at[(r // 2) % 2, (c // 2) % 2, r // 4, c // 4],
            c_send.at[n],
            c_recv.at[4 * (r // 4) + c // 4],
            rr,
            cc,
        )

    def three_landing(n):
        return remote(t3, m3.at[r % 2, c % 2, n // 4, n % 4], c_send.at[n], c_recv.at[n], r, c)

    def is_other(n):
        rr, cc = partner(n)
        return (rr != r) | (cc != c)

    def over_partners(act):
        def step(n, _):
            @pl.when(is_other(n))
            def _():
                act(n)

            return 0

        lax.fori_loop(0, 16, step, 0)

    over_partners(lambda n: three_copy(n).start())

    @pl.when((swap(r % 4) == r % 4) & (swap(c % 4) == c % 4))
    def _():
        m3[r % 2, c % 2, r // 4, c // 4] = t3[...]

    each(four_copy, 2, sends_to, lambda copy: copy.start())

    for dx in (2, 3, 4):
        turn(dx)

    over_partners(lambda n: three_landing(n).wait_recv())

    def share_copy(n):
        dr, dc = MATES[n]
        part = m3.at[r % 2, c % 2]
        return remote(
            part, part, d_send.at[n], d_recv.at[n], r + dr * (1 - 2 * (r % 2)), c + dc * (1 - 2 * (c % 2))
        )

    def share_landing(n):
        dr, dc = MATES[n]
        part = m3.at[(r + dr) % 2, (c + dc) % 2]
        return remote(part, part, d_send.at[n], d_recv.at[n], r, c)

    for n in range(3):
        share_copy(n).start()
    for dx in (5, 6):
        turn(dx)
    for n in range(3):
        share_landing(n).wait_recv()

    for b in range(2):
        for i in range(4):
            for a in range(2):
                n3[b, a, 64 * i : 64 * i + 64] = jnp.concatenate(
                    [m3[a, b, i, j].astype(F32) for j in range(4)], axis=0
                )
    total = jnp.zeros((128, 128), F32)
    for b in range(2):
        for cz in range(2):
            rows = jnp.concatenate(
                [n3[b, a, pl.ds(cz, 128, stride=2), :] for a in range(2)], axis=1
            )
            total = total + dot(rows.astype(BF16), wm[2 * b + cz])
    for n in range(16):
        n2[n // 4, n % 4] = total[8 * n : 8 * n + 8]

    each(four_copy, 2, gets_from, lambda copy: copy.wait_recv())
    each(five_copy, 1, gets_from, lambda copy: copy.wait_recv())
    row8 = lax.broadcasted_iota(jnp.int32, (8, 256), 0)
    from_below = (row8 == 1) | (row8 == 2) | (row8 == 3) | (row8 == 5)
    from_above = (row8 == 0) | (row8 == 1) | (row8 == 2) | (row8 == 4)

    def wide(ref, k):
        return jnp.concatenate([ref[a, pl.ds(k, 8, stride=6), :] for a in range(2)], axis=1)

    def levels(column, below, above):
        v = [column(k) for k in range(6)]
        low = [jnp.where(below, pltpu.roll(v[k], 1, axis=0), 0.0) for k in (4, 5)]
        high = [jnp.where(above, pltpu.roll(v[k], 7, axis=0), 0.0) for k in (0, 1)]
        return low + v + high

    def coarse(n, _):
        x, y = n // 6, n % 6
        half, odd = y // 2, y % 2
        five = w5[x, half].astype(F32)
        five = jnp.where(odd == 0, five[0:24], five[24:48])
        i3, j3 = r // 4 - 1 + x, c // 4 - 1 + half
        ok3 = (i3 >= 0) & (i3 < 4) & (j3 >= 0) & (j3 < 4)
        j2 = 2 * (c // 8) - 2 + y
        for a in range(2):
            nat[a, 0:24] = five[:, 128 * a : 128 * a + 128]
            nat[a, 24:36] = w4[x, half, a, odd].astype(F32)[0:12]
            three = m3[a, odd, jnp.clip(i3, 0, 3), jnp.clip(j3, 0, 3)].astype(F32)
            nat[a, 36:42] = jnp.where(ok3, three[0:6], 0.0)
            i2 = 2 * (r // 8 - 1 + x) + a
            ok2 = (i2 >= 0) & (i2 < 4) & (j2 >= 0) & (j2 < 4)
            two = n2[jnp.clip(i2, 0, 3), jnp.clip(j2, 0, 3)]
            nat[a, 42:48] = jnp.where(ok2, two[0:6], 0.0)
        v = levels(lambda k: wide(nat, k), from_below, from_above)
        for s in range(6):
            ts[x, y, s] = jnp.concatenate(
                [v[s], v[s + 2], v[s + 4], jnp.zeros((8, 256), F32)], axis=0
            ).astype(BF16)
        return 0

    lax.fori_loop(0, 18, coarse, 0)

    each(rim_copy, 1, gets_from, lambda copy: copy.wait_recv())

    def fine(y, _):
        before = None
        for x in range(4):
            whole = w6[x, y].astype(F32)
            for a in range(2):
                col[x, a] = whole[:, 128 * a : 128 * a + 128]
            v = levels(lambda k: wide(col.at[x], k), row8 >= 1, row8 <= 6)
            if before is not None:
                for k in range(10):
                    t6[x - 1, y, k] = jnp.concatenate([before[k], v[k]], axis=0).astype(BF16)
            before = v
        return 0

    lax.fori_loop(0, 8, fine, 0)

    def far(p, _):
        py, pz = p // 2, p % 2
        near = [-1, 0, 1, -2, 2]
        total = jnp.zeros((128, 256), F32)
        for j in range(3):
            for ey in range(6):
                dy = near[ey] if ey < 5 else 3 - 6 * py
                for ez in range(6):
                    dz = near[ez] if ez < 5 else 3 - 6 * pz
                    if j == 1 and ey < 3 and ez < 3:
                        continue
                    y0, k0 = py + dy + 2, pz + dz + 2
                    x = jnp.concatenate(
                        [t6[j, y0 + 2 * t, k0 + 2 * m] for t in range(2) for m in range(3)]
                        + [ts[j, y0, k0]],
                        axis=0,
                    )
                    w = jnp.concatenate(
                        [
                            jnp.concatenate(
                                [opt[2 * j + a - 2 - px + 3, dy + 3, dz + 3] for px in range(2)],
                                axis=1,
                            )
                            for a in range(2)
                        ],
                        axis=0,
                    )
                    total = total + dot(x, w)
        for px in range(2):
            lanes = slice(128 * px, 128 * px + 128)
            for m in range(3):
                zs = pl.ds(2 * m + pz, 8, stride=6)
                for t in range(2):
                    for g in range(2):
                        at = 48 * t + 16 * m + 8 * g
                        f6[2 * g + px, py + 2 * t, zs, :] = total[at : at + 8, lanes]
                fs[px, py, zs, :] = total[96 + 8 * m : 104 + 8 * m, lanes]
        return 0

    lax.fori_loop(0, 4, far, 0)

    def refine(parents, a, b):
        return dot(parents.astype(BF16), wl[2 * a + b])

    ls[...] = jnp.zeros_like(ls)
    two = fs[(r // 4) % 2, (c // 4) % 2, 40:48, :]
    ls[0, 0:8] = two
    two = jnp.concatenate([ls[0, 2:8], jnp.zeros((10, 128), F32)], axis=0)
    both = refine(two, (r // 2) % 2, (c // 2) % 2)
    for cz in range(2):
        ls[1, pl.ds(cz, 8, stride=2), :] = both[0:8, 128 * cz : 128 * cz + 128]
    three = ls[1, 0:6] + fs[(r // 2) % 2, (c // 2) % 2, 36:42, :]
    three = jnp.concatenate([three, jnp.zeros((10, 128), F32)], axis=0)
    both = refine(three, r % 2, c % 2)
    for cz in range(2):
        ls[2, pl.ds(cz, 8, stride=2), :] = both[0:8, 128 * cz : 128 * cz + 128]
    four = ls[2, 0:12] + fs[r % 2, c % 2, 24:36, :]
    four = jnp.concatenate([four, jnp.zeros((4, 128), F32)], axis=0)
    fives = []
    for a in range(2):
        for b in range(2):
            both = refine(four, a, b)
            for cz in range(2):
                ls[3 + 2 * a + b, pl.ds(cz, 16, stride=2), :] = both[:, 128 * cz : 128 * cz + 128]
            fives.append(ls[3 + 2 * a + b, 0:24] + fs[a, b, 0:24, :])
    five = jnp.concatenate(fives, axis=0).astype(BF16)
    for a in range(2):
        for b in range(2):
            both = dot(five, wl[2 * a + b])
            for x in range(2):
                for y in range(2):
                    at = 24 * (2 * x + y)
                    for cz in range(2):
                        zs = pl.ds(cz, 24, stride=2)
                        s6[2 * x + a, 2 * y + b, zs, :] = (
                            f6[2 * x + a, 2 * y + b, zs, :]
                            + both[at : at + 24, 128 * cz : 128 * cz + 128]
                        )
    out[...] = s6[:, :, :, 0:C]

    for n in range(3):
        mate_copy(n).wait_send()
        share_copy(n).wait_send()
    each(five_copy, 1, sends_to, lambda copy: copy.wait_send())
    each(rim_copy, 1, sends_to, lambda copy: copy.wait_send())
    each(four_copy, 2, sends_to, lambda copy: copy.wait_send())
    over_partners(lambda n: three_copy(n).wait_send())


def local(leaf_multipoles, occupancy, m2m_ops, m2l_ops, l2l_ops):
    leaf = jnp.transpose(leaf_multipoles, (1, 2, 3, 0))
    pad = 128 - C
    wm = jnp.pad(
        jnp.transpose(m2m_ops, (1, 2, 0, 4, 3)), ((0, 0),) * 3 + ((0, pad), (0, pad))
    ).reshape(4, 256, 128)
    wl = jnp.pad(
        jnp.transpose(l2l_ops, (0, 1, 4, 2, 3)), ((0, 0),) * 2 + ((0, pad), (0, 0), (0, pad))
    ).reshape(4, 128, 256)
    vmem = pl.BlockSpec(memory_space=pltpu.VMEM)
    dma = pltpu.SemaphoreType.DMA
    result = pl.pallas_call(
        kernel,
        out_shape=jax.ShapeDtypeStruct((4, 4, 48, C), F32),
        in_specs=[vmem] * 4 + [pl.BlockSpec(memory_space=pl.ANY)],
        out_specs=vmem,
        scratch_shapes=[
            pltpu.VMEM((7, 7, 7, C, C), BF16),
            pltpu.VMEM((7, 7, 7, 128, 128), BF16),
            pltpu.VMEM((4, 4, 48, 128), F32),
            pltpu.VMEM((4, 8, 48, 256), BF16),
            pltpu.VMEM((2, 64, 128), F32),
            pltpu.VMEM((3, 3, 48, 256), BF16),
            pltpu.VMEM((3, 3, 2, 2, 16, 128), BF16),
            pltpu.VMEM((2, 2, 16, 128), F32),
            pltpu.VMEM((16, 128), BF16),
            pltpu.VMEM((2, 2, 4, 4, 16, 128), BF16),
            pltpu.VMEM((2, 2, 256, 128), F32),
            pltpu.VMEM((4, 4, 8, 128), F32),
            pltpu.VMEM((2, 48, 128), F32),
            pltpu.VMEM((4, 2, 48, 128), F32),
            pltpu.VMEM((3, 8, 10, 16, 256), BF16),
            pltpu.VMEM((3, 6, 6, 32, 256), BF16),
            pltpu.VMEM((4, 4, 48, 128), F32),
            pltpu.VMEM((2, 2, 48, 128), F32),
            pltpu.VMEM((7, 32, 128), F32),
            dma((7,)),
            dma((8,)),
            dma((8,)),
            dma((8,)),
            dma((8,)),
            dma((3,)),
            dma((3,)),
            dma((8,)),
            dma((8,)),
            dma((16,)),
            dma((16,)),
            dma((3,)),
            dma((3,)),
        ],
        compiler_params=pltpu.CompilerParams(
            collective_id=0, has_side_effects=True, vmem_limit_bytes=56 * 2**20
        ),
    )(leaf, occupancy, wm, wl, m2l_ops)
    return jnp.transpose(result, (3, 0, 1, 2))


def solution(mesh):
    placed = (P(None, "row", "col", None), P("row", "col", None), P(), P(), P())
    return jax.shard_map(
        local, mesh=mesh, in_specs=placed, out_specs=P(None, "row", "col", None), check_vma=False
    )
```

profile of v0, /device:TPU:1, one launch (start us, length us, event | category | flops | bytes accessed | tf_op | source)
XLA Modules:
  0.0 57.6 jit_solution(13550199857605275808)
XLA Ops:
  0.0 1.2 %copy.9 = bf16[2,2,121,2,121]{4,3,2,1,0:T(2,128)(2,1)S(1)} copy(bf16[2,2,121,2,121]{2,3,4,1,0:T(2,128)(2,1)} %bitcast.8) | data formatting | bytes 468512
  1.2 0.3 pad.9.clone
  1.5 0.9 %reshape.7.wl = bf16[4,128,256]{2,1,0:T(8,128)(2,1)} reshape(bf16[2,2,128,2,128]{4,3,2,1,0:T(2,128)(2,1)S(1)} %pad.9.clone) | data formatting | bytes 524288 | tf_op jit(solution)/shard_map/reshape | solution.py:494
  2.4 1.2 %copy.8 = bf16[2,2,2,121,121]{4,3,2,1,0:T(8,128)(2,1)S(1)} copy(bf16[2,2,2,121,121]{3,1,4,0,2:T(2,128)(2,1)} %bitcast.9) | data formatting | bytes 468512
  3.5 0.8 %pad.8.clone = bf16[2,2,2,128,128]{4,3,2,1,0:T(8,128)(2,1)} pad(bf16[2,2,2,121,121]{4,3,2,1,0:T(8,128)(2,1)S(1)} %copy.8, bf16[]{:T(256)} %constant.2.clone.1), padding=0_0x0_0x0_0x0_7x0_7 | pad | bytes 496402 | tf_op jit(solution)/shard_map/jit(_pad)/pad | solution.py:489
  4.3 51.5 %shard_map.55 = f32[4,4,48,121]{3,2,1,0:T(8,128)} custom-call(f32[4,4,48,121]{3,2,1,0:T(8,128)} %bitcast.7, s32[4,4,48]{2,1,0:T(4,128)} %occ.1, bf16[4,256,128]{2,1,0:T(8,128)(2,1)} %bitcast.6, bf16[4,128,256]{2,1,0:T(8,128)(2,1)} %reshape.7.wl, bf16[7,7,7,121,121]{4,3,2,1,0:T(8,128)(2,1)} %ops_hbm.1), custom_call_target="tpu_custom_call" | custom-call | tf_op jit(solution)/shard_map/pallas_call | solution.py:497
  55.8 1.8 %copy.11 = f32[121,4,4,48]{0,3,2,1:T(8,128)} copy(f32[121,4,4,48]{0,3,2,1:T(8,128)} %bitcast.5) | data formatting | bytes 743424
where the time goes:
time: 58 us; the launch traced here: 57.6 us
  Pallas kernels  51.5 us (89%)
  local copies, waits for them, and re-layouts  6.06 us (10%)
    pallas_call x1, Pallas kernels, local(): pl.pallas_call(kernel, out_shape=jax.ShapeDtypeStruct((4, 4, 48, C), F32)...  51.5 us
    unnamed x3, local copies, waits for them, and re-layouts  4.16 us

commit v1 on v0

--- a/solution.py
+++ b/solution.py
@@ -24,9 +24,9 @@
 
 
 def kernel(
-    leaf, occ, wm, wl, ops_hbm,
+    leaf, occ, m2m, l2l, ops_hbm,
     out,
-    ops, opt, s6, w6, n5, w5, w4, n4, t3, m3, n3, n2, nat, col, t6, ts, f6, fs, ls,
+    ops, opt, mf, wm, lf, wl, s6, w6, n5, w5, w4, n4, t3, m3, n3, n2, nat, col, t6, ts, f6, fs, ls,
     ops_sem, s6_send, s6_recv, s5_send, s5_recv, a_send, a_recv, b_send, b_recv,
     c_send, c_recv, d_send, d_recv,
 ):
@@ -83,6 +83,17 @@
         for y in range(4):
             for a in range(2):
                 w6[1 + x, 2 + y, :, a * 128 : (a + 1) * 128] = s6[2 * x + a, y].astype(BF16)
+
+    def octant(raw, a, b, cz):
+        rows = raw[pl.ds((2 * a + b) * 2 * C + cz, 128, stride=2), :]
+        return jnp.transpose(rows)[0:C, 0:C].astype(BF16)
+
+    mf[0 : 8 * C, 0:C] = m2m[...].astype(F32)
+    wm[...] = jnp.zeros_like(wm)
+    for a in range(2):
+        for b in range(2):
+            for cz in range(2):
+                wm[2 * b + cz, 128 * a : 128 * a + C, 0:C] = octant(mf, a, b, cz)
 
     total = jnp.zeros((96, 128), F32)
     for b in range(2):
@@ -219,26 +230,23 @@
     each(five_copy, 1, sends_to, lambda copy: copy.start())
     each(rim_copy, 1, sends_to, lambda copy: copy.start())
 
-    opt_pad = jnp.zeros((7, 128), BF16)
-    opt_side = jnp.zeros((128, 7), BF16)
-
     def turn(dx):
         ops_copies[dx].wait()
 
-        def one(n, _):
-            dy, dz = n // 7, n % 7
-            block = jnp.concatenate(
-                [jnp.concatenate([ops[dx, dy, dz], opt_pad[:, 0:C]], axis=0), opt_side], axis=1
-            )
-            opt[dx, dy, dz] = jnp.transpose(block)
-            return 0
-
-        lax.fori_loop(0, 49, one, 0)
-        if 2 <= dx <= 4:
-            for dy in range(2, 5):
-                for dz in range(2, 5):
+        for dy in range(7):
+            for dz in range(7):
+                if all(2 <= d <= 4 for d in (dx, dy, dz)):
                     opt[dx, dy, dz] = jnp.zeros((128, 128), BF16)
-
+                else:
+                    opt[dx, dy, dz, 112:128] = jnp.zeros((16, 128), BF16)
+                    opt[dx, dy, dz, 0:C, 0:C] = jnp.transpose(ops[dx, dy, dz])
+
+    lf[0 : 8 * C, 0:C] = l2l[...].astype(F32)
+    wl[...] = jnp.zeros_like(wl)
+    for a in range(2):
+        for b in range(2):
+            for cz in range(2):
+                wl[2 * a + b, 0:C, 128 * cz : 128 * cz + C] = octant(lf, a, b, cz)
     for dx in (0, 1):
         turn(dx)
 
@@ -435,8 +443,12 @@
 
     lax.fori_loop(0, 4, far, 0)
 
+    def real(parents):
+        lane = lax.broadcasted_iota(jnp.int32, parents.shape, 1)
+        return jnp.where(lane < C, parents, 0.0).astype(BF16)
+
     def refine(parents, a, b):
-        return dot(parents.astype(BF16), wl[2 * a + b])
+        return dot(real(parents), wl[2 * a + b])
 
     ls[...] = jnp.zeros_like(ls)
     two = fs[(r // 4) % 2, (c // 4) % 2, 40:48, :]
@@ -459,7 +471,7 @@
             for cz in range(2):
                 ls[3 + 2 * a + b, pl.ds(cz, 16, stride=2), :] = both[:, 128 * cz : 128 * cz + 128]
             fives.append(ls[3 + 2 * a + b, 0:24] + fs[a, b, 0:24, :])
-    five = jnp.concatenate(fives, axis=0).astype(BF16)
+    five = real(jnp.concatenate(fives, axis=0))
     for a in range(2):
         for b in range(2):
             both = dot(five, wl[2 * a + b])
@@ -485,13 +497,8 @@
 
 def local(leaf_multipoles, occupancy, m2m_ops, m2l_ops, l2l_ops):
     leaf = jnp.transpose(leaf_multipoles, (1, 2, 3, 0))
-    pad = 128 - C
-    wm = jnp.pad(
-        jnp.transpose(m2m_ops, (1, 2, 0, 4, 3)), ((0, 0),) * 3 + ((0, pad), (0, pad))
-    ).reshape(4, 256, 128)
-    wl = jnp.pad(
-        jnp.transpose(l2l_ops, (0, 1, 4, 2, 3)), ((0, 0),) * 2 + ((0, pad), (0, 0), (0, pad))
-    ).reshape(4, 128, 256)
+    m2m = jnp.transpose(m2m_ops, (0, 1, 3, 2, 4)).reshape(8 * C, C)
+    l2l = jnp.transpose(l2l_ops, (0, 1, 3, 2, 4)).reshape(8 * C, C)
     vmem = pl.BlockSpec(memory_space=pltpu.VMEM)
     dma = pltpu.SemaphoreType.DMA
     result = pl.pallas_call(
@@ -502,6 +509,10 @@
         scratch_shapes=[
             pltpu.VMEM((7, 7, 7, C, C), BF16),
             pltpu.VMEM((7, 7, 7, 128, 128), BF16),
+            pltpu.VMEM((984, 128), F32),
+            pltpu.VMEM((4, 256, 128), BF16),
+            pltpu.VMEM((984, 128), F32),
+            pltpu.VMEM((4, 128, 256), BF16),
             pltpu.VMEM((4, 4, 48, 128), F32),
             pltpu.VMEM((4, 8, 48, 256), BF16),
             pltpu.VMEM((2, 64, 128), F32),
@@ -536,7 +547,7 @@
         compiler_params=pltpu.CompilerParams(
             collective_id=0, has_side_effects=True, vmem_limit_bytes=56 * 2**20
         ),
-    )(leaf, occupancy, wm, wl, m2l_ops)
+    )(leaf, occupancy, m2m, l2l, m2l_ops)
     return jnp.transpose(result, (3, 0, 1, 2))
 
 

time: 58 us -> 42.3 us (0.73)
  Pallas kernels: 51.5 us -> 39.7 us
  local copies, waits for them, and re-layouts: 6.06 us -> 1.77 us
    pallas_call x1, Pallas kernels: 51.5 us -> 39.7 us  [local(): pl.pallas_call(kernel, out_shape=jax.ShapeDtypeStruct((4, 4, 48, C), F32)...]
    unnamed x3 -> x1, local copies, waits for them, and re-layouts: 4.16 us -> 1.77 us
    pad x2 -> x0, local copies, waits for them, and re-layouts: 1.03 us -> none  [the longest x1 0.77 us: local(): jnp.pad(jnp.transpose(m2m_ops, (1, 2, 0, 4, 3)), ((0, 0),) * 3 + ((0, pad...]
    reshape x1 -> x0, local copies, waits for them, and re-layouts: 0.87 us -> none  [local(): wl = jnp.pad(jnp.transpose(l2l_ops, (0, 1, 4, 2, 3)), ((0, 0),) * 2 + ((0...]
where the time goes in v1:
time: 42.3 us; the launch traced here: 41.5 us
  Pallas kernels  39.7 us (94%)
  local copies, waits for them, and re-layouts  1.77 us (4%)
    pallas_call x1, Pallas kernels, local(): pl.pallas_call(kernel, out_shape=jax.ShapeDtypeStruct((4, 4, 48, C), F32)...  39.7 us
    unnamed x1, local copies, waits for them, and re-layouts  1.77 us

profile of v1, /device:TPU:1, one launch (start us, length us, event | category | flops | bytes accessed | tf_op | source)
XLA Modules:
  0.0 41.5 jit_solution(10272165365937974636)
XLA Ops:
  0.0 39.7 %shard_map.55 = f32[4,4,48,121]{3,2,1,0:T(8,128)} custom-call(f32[4,4,48,121]{3,2,1,0:T(8,128)} %bitcast.9, s32[4,4,48]{2,1,0:T(4,128)} %occ.1, bf16[968,121]{1,0:T(8,128)(2,1)} %bitcast.10, bf16[968,121]{1,0:T(8,128)(2,1)} %bitcast.11, bf16[7,7,7,121,121]{4,3,2,1,0:T(8,128)(2,1)} %ops_hbm.1), custom_call_target="tpu_custom_call" | custom-call | tf_op jit(solution)/shard_map/pallas_call | solution.py:504
  39.8 1.8 %copy.7 = f32[121,4,4,48]{0,3,2,1:T(8,128)} copy(f32[121,4,4,48]{0,3,2,1:T(8,128)} %bitcast.8) | data formatting | bytes 743424

commit v2 on v1

--- a/solution.py
+++ b/solution.py
@@ -26,7 +26,7 @@
 def kernel(
     leaf, occ, m2m, l2l, ops_hbm,
     out,
-    ops, opt, mf, wm, lf, wl, s6, w6, n5, w5, w4, n4, t3, m3, n3, n2, nat, col, t6, ts, f6, fs, ls,
+    ops, opt, mf, wm, lf, wl, s6, w6, n5, w5, w4, n4, t3, m3, n3, n2, nat, col, t6, ts, acc, acs, f6, fs, ls,
     ops_sem, s6_send, s6_recv, s5_send, s5_recv, a_send, a_recv, b_send, b_recv,
     c_send, c_recv, d_send, d_recv,
 ):
@@ -218,8 +218,8 @@
         dr, dc = AROUND[n]
         return inside(r - scale * dr, c - scale * dc)
 
-    def each(make, scale, wanted, act):
-        for n in range(8):
+    def each(make, scale, wanted, act, which=range(8)):
+        for n in which:
 
             @pl.when(wanted(n, scale))
             def _():
@@ -227,8 +227,19 @@
 
     for n in range(3):
         mate_copy(n).start()
-    each(five_copy, 1, sends_to, lambda copy: copy.start())
-    each(rim_copy, 1, sends_to, lambda copy: copy.start())
+    SIDES = [n for n in range(8) if AROUND[n][0] == 0]
+    ENDS = [n for n in range(8) if AROUND[n][1] == 0]
+    CORNERS = [n for n in range(8) if AROUND[n][0] != 0 and AROUND[n][1] != 0]
+
+    def start(copy):
+        copy.start()
+
+    def wait_recv(copy):
+        copy.wait_recv()
+
+    each(rim_copy, 1, sends_to, start, ENDS)
+    each(five_copy, 1, sends_to, start)
+    each(rim_copy, 1, sends_to, start, SIDES + CORNERS)
 
     def turn(dx):
         ops_copies[dx].wait()
@@ -247,6 +258,9 @@
         for b in range(2):
             for cz in range(2):
                 wl[2 * a + b, 0:C, 128 * cz : 128 * cz + C] = octant(lf, a, b, cz)
+    acc[...] = jnp.zeros_like(acc)
+    acs[...] = jnp.zeros_like(acs)
+    ls[...] = jnp.zeros_like(ls)
     for dx in (0, 1):
         turn(dx)
 
@@ -304,7 +318,7 @@
 
     each(four_copy, 2, sends_to, lambda copy: copy.start())
 
-    for dx in (2, 3, 4):
+    for dx in (2, 3, 4, 5, 6):
         turn(dx)
 
     over_partners(lambda n: three_landing(n).wait_recv())
@@ -323,8 +337,76 @@
 
     for n in range(3):
         share_copy(n).start()
-    for dx in (5, 6):
-        turn(dx)
+    row8 = lax.broadcasted_iota(jnp.int32, (8, 256), 0)
+    from_below = (row8 == 1) | (row8 == 2) | (row8 == 3) | (row8 == 5)
+    from_above = (row8 == 0) | (row8 == 1) | (row8 == 2) | (row8 == 4)
+
+    def wide(ref, k):
+        return jnp.concatenate([ref[a, pl.ds(k, 8, stride=6), :] for a in range(2)], axis=1)
+
+    def levels(column, below, above):
+        v = [column(k) for k in range(6)]
+        low = [jnp.where(below, pltpu.roll(v[k], 1, axis=0), 0.0) for k in (4, 5)]
+        high = [jnp.where(above, pltpu.roll(v[k], 7, axis=0), 0.0) for k in (0, 1)]
+        return low + v + high
+
+    def fine(x, y):
+        whole = w6[x, y].astype(F32)
+        for a in range(2):
+            col[x, a] = whole[:, 128 * a : 128 * a + 128]
+        return levels(lambda k: wide(col.at[x], k), row8 >= 1, row8 <= 6)
+
+    def pair(x, y):
+        low, high = fine(x, y), fine(x + 1, y)
+        for k in range(10):
+            t6[x, y, k] = jnp.concatenate([low[k], high[k]], axis=0).astype(BF16)
+
+    def pairs(xs, ys):
+        def step(n, _):
+            for x in xs:
+                pair(x, ys(n))
+            return 0
+
+        return step
+
+    def far(own, small):
+        for dy in range(-3, 4):
+            for dz in range(-3, 4):
+                use = [j for j in range(3) if j != 1 or max(abs(dy), abs(dz)) > 1]
+                tys = range(4) if abs(dy) < 3 else (0, 2) if dy > 0 else (1, 3)
+                tys = [ty for ty in tys if (0 <= ty + dy <= 3) == own]
+                if not tys and not small:
+                    continue
+                tks = range(6) if abs(dz) < 3 else (0, 2, 4) if dz > 0 else (1, 3, 5)
+                w = jnp.concatenate(
+                    [
+                        jnp.concatenate(
+                            [opt[2 * j + a - px + 1, dy + 3, dz + 3] for px in range(2)], axis=1
+                        )
+                        for j in use
+                        for a in range(2)
+                    ],
+                    axis=0,
+                )
+                rows, sums = [], []
+                for ty in tys:
+                    for k in tks:
+                        rows.append([t6[j, ty + dy + 2, k + dz + 2] for j in use])
+                        sums.append(acc.at[ty, k])
+                if small:
+                    for k in tks:
+                        rows.append([ts[j, dy + 3, k + dz + 2] for j in use])
+                        sums.append(acs.at[k])
+                total = dot(
+                    jnp.concatenate([jnp.concatenate(row, axis=1) for row in rows], axis=0), w
+                )
+                for n, tile in enumerate(sums):
+                    tile[...] += total[16 * n : 16 * n + 16]
+
+
+    each(rim_copy, 1, gets_from, wait_recv, ENDS)
+    lax.fori_loop(2, 6, pairs([0, 1, 2], lambda n: n), 0)
+    far(True, False)
     for n in range(3):
         share_landing(n).wait_recv()
 
@@ -346,24 +428,10 @@
 
     each(four_copy, 2, gets_from, lambda copy: copy.wait_recv())
     each(five_copy, 1, gets_from, lambda copy: copy.wait_recv())
-    row8 = lax.broadcasted_iota(jnp.int32, (8, 256), 0)
-    from_below = (row8 == 1) | (row8 == 2) | (row8 == 3) | (row8 == 5)
-    from_above = (row8 == 0) | (row8 == 1) | (row8 == 2) | (row8 == 4)
-
-    def wide(ref, k):
-        return jnp.concatenate([ref[a, pl.ds(k, 8, stride=6), :] for a in range(2)], axis=1)
-
-    def levels(column, below, above):
-        v = [column(k) for k in range(6)]
-        low = [jnp.where(below, pltpu.roll(v[k], 1, axis=0), 0.0) for k in (4, 5)]
-        high = [jnp.where(above, pltpu.roll(v[k], 7, axis=0), 0.0) for k in (0, 1)]
-        return low + v + high
-
-    def coarse(n, _):
-        x, y = n // 6, n % 6
+    def coarse(x, y):
         half, odd = y // 2, y % 2
         five = w5[x, half].astype(F32)
-        five = jnp.where(odd == 0, five[0:24], five[24:48])
+        five = five[24 * odd : 24 * odd + 24]
         i3, j3 = r // 4 - 1 + x, c // 4 - 1 + half
         ok3 = (i3 >= 0) & (i3 < 4) & (j3 >= 0) & (j3 < 4)
         j2 = 2 * (c // 8) - 2 + y
@@ -376,72 +444,32 @@
             ok2 = (i2 >= 0) & (i2 < 4) & (j2 >= 0) & (j2 < 4)
             two = n2[jnp.clip(i2, 0, 3), jnp.clip(j2, 0, 3)]
             nat[a, 42:48] = jnp.where(ok2, two[0:6], 0.0)
-        v = levels(lambda k: wide(nat, k), from_below, from_above)
-        for s in range(6):
-            ts[x, y, s] = jnp.concatenate(
-                [v[s], v[s + 2], v[s + 4], jnp.zeros((8, 256), F32)], axis=0
-            ).astype(BF16)
+        return levels(lambda k: wide(nat, k), from_below, from_above)
+
+    def small_windows(x, _):
+        nothing = [jnp.zeros((8, 256), F32)] * 10
+        before = nothing
+        for y in range(7):
+            now = coarse(x, y) if y < 6 else nothing
+            for k in range(10):
+                ts[x, y, k] = jnp.concatenate([before[k], now[k]], axis=0).astype(BF16)
+            before = now
         return 0
 
-    lax.fori_loop(0, 18, coarse, 0)
-
-    each(rim_copy, 1, gets_from, lambda copy: copy.wait_recv())
-
-    def fine(y, _):
-        before = None
-        for x in range(4):
-            whole = w6[x, y].astype(F32)
-            for a in range(2):
-                col[x, a] = whole[:, 128 * a : 128 * a + 128]
-            v = levels(lambda k: wide(col.at[x], k), row8 >= 1, row8 <= 6)
-            if before is not None:
-                for k in range(10):
-                    t6[x - 1, y, k] = jnp.concatenate([before[k], v[k]], axis=0).astype(BF16)
-            before = v
-        return 0
-
-    lax.fori_loop(0, 8, fine, 0)
-
-    def far(p, _):
-        py, pz = p // 2, p % 2
-        near = [-1, 0, 1, -2, 2]
-        total = jnp.zeros((128, 256), F32)
-        for j in range(3):
-            for ey in range(6):
-                dy = near[ey] if ey < 5 else 3 - 6 * py
-                for ez in range(6):
-                    dz = near[ez] if ez < 5 else 3 - 6 * pz
-                    if j == 1 and ey < 3 and ez < 3:
-                        continue
-                    y0, k0 = py + dy + 2, pz + dz + 2
-                    x = jnp.concatenate(
-                        [t6[j, y0 + 2 * t, k0 + 2 * m] for t in range(2) for m in range(3)]
-                        + [ts[j, y0, k0]],
-                        axis=0,
-                    )
-                    w = jnp.concatenate(
-                        [
-                            jnp.concatenate(
-                                [opt[2 * j + a - 2 - px + 3, dy + 3, dz + 3] for px in range(2)],
-                                axis=1,
-                            )
-                            for a in range(2)
-                        ],
-                        axis=0,
-                    )
-                    total = total + dot(x, w)
+    lax.fori_loop(0, 3, small_windows, 0)
+
+    each(rim_copy, 1, gets_from, wait_recv, SIDES + CORNERS)
+    lax.fori_loop(0, 4, pairs([0, 1, 2], lambda n: n + 4 * (n // 2)), 0)
+    far(False, True)
+    for k in range(6):
+        zs = pl.ds(k, 8, stride=6)
         for px in range(2):
             lanes = slice(128 * px, 128 * px + 128)
-            for m in range(3):
-                zs = pl.ds(2 * m + pz, 8, stride=6)
-                for t in range(2):
-                    for g in range(2):
-                        at = 48 * t + 16 * m + 8 * g
-                        f6[2 * g + px, py + 2 * t, zs, :] = total[at : at + 8, lanes]
-                fs[px, py, zs, :] = total[96 + 8 * m : 104 + 8 * m, lanes]
-        return 0
-
-    lax.fori_loop(0, 4, far, 0)
+            for g in range(2):
+                for ty in range(4):
+                    f6[2 * g + px, ty, zs, :] = acc[ty, k, 8 * g : 8 * g + 8, lanes]
+            for py in range(2):
+                fs[px, py, zs, :] = acs[k, 8 * py : 8 * py + 8, lanes]
 
     def real(parents):
         lane = lax.broadcasted_iota(jnp.int32, parents.shape, 1)
@@ -450,7 +478,6 @@
     def refine(parents, a, b):
         return dot(real(parents), wl[2 * a + b])
 
-    ls[...] = jnp.zeros_like(ls)
     two = fs[(r // 4) % 2, (c // 4) % 2, 40:48, :]
     ls[0, 0:8] = two
     two = jnp.concatenate([ls[0, 2:8], jnp.zeros((10, 128), F32)], axis=0)
@@ -526,7 +553,9 @@
             pltpu.VMEM((2, 48, 128), F32),
             pltpu.VMEM((4, 2, 48, 128), F32),
             pltpu.VMEM((3, 8, 10, 16, 256), BF16),
-            pltpu.VMEM((3, 6, 6, 32, 256), BF16),
+            pltpu.VMEM((3, 7, 10, 16, 256), BF16),
+            pltpu.VMEM((4, 6, 16, 256), F32),
+            pltpu.VMEM((6, 16, 256), F32),
             pltpu.VMEM((4, 4, 48, 128), F32),
             pltpu.VMEM((2, 2, 48, 128), F32),
             pltpu.VMEM((7, 32, 128), F32),

time: 42.3 us -> 40.3 us (0.953); the launches traced: 41.5 us -> 40.2 us
  Pallas kernels: 39.7 us -> 38.4 us
    pallas_call x1, Pallas kernels: 39.7 us -> 38.4 us  [local(): pl.pallas_call(kernel, out_shape=jax.ShapeDtypeStruct((4, 4, 48, C), F32)...]
where the time goes in v2:
time: 40.3 us; the launch traced here: 40.2 us
  Pallas kernels  38.4 us (95%)
  local copies, waits for them, and re-layouts  1.77 us (4%)
    pallas_call x1, Pallas kernels, local(): pl.pallas_call(kernel, out_shape=jax.ShapeDtypeStruct((4, 4, 48, C), F32)...  38.4 us
    unnamed x1, local copies, waits for them, and re-layouts  1.77 us

profile of v2, /device:TPU:1, one launch (start us, length us, event | category | flops | bytes accessed | tf_op | source)
XLA Modules:
  0.0 40.2 jit_solution(13054734214241744708)
XLA Ops:
  0.0 38.4 %shard_map.55 = f32[4,4,48,121]{3,2,1,0:T(8,128)} custom-call(f32[4,4,48,121]{3,2,1,0:T(8,128)} %bitcast.9, s32[4,4,48]{2,1,0:T(4,128)} %occ.1, bf16[968,121]{1,0:T(8,128)(2,1)} %bitcast.10, bf16[968,121]{1,0:T(8,128)(2,1)} %bitcast.11, bf16[7,7,7,121,121]{4,3,2,1,0:T(8,128)(2,1)} %ops_hbm.1), custom_call_target="tpu_custom_call" | custom-call | tf_op jit(solution)/shard_map/pallas_call | solution.py:531
  38.4 1.8 %copy.7 = f32[121,4,4,48]{0,3,2,1:T(8,128)} copy(f32[121,4,4,48]{0,3,2,1:T(8,128)} %bitcast.8) | data formatting | bytes 743424

commit v3 on v2

--- a/solution.py
+++ b/solution.py
@@ -237,9 +237,7 @@
     def wait_recv(copy):
         copy.wait_recv()
 
-    each(rim_copy, 1, sends_to, start, ENDS)
-    each(five_copy, 1, sends_to, start)
-    each(rim_copy, 1, sends_to, start, SIDES + CORNERS)
+    each(rim_copy, 1, sends_to, start, SIDES + ENDS)
 
     def turn(dx):
         ops_copies[dx].wait()
@@ -311,6 +309,8 @@
         lax.fori_loop(0, 16, step, 0)
 
     over_partners(lambda n: three_copy(n).start())
+    each(rim_copy, 1, sends_to, start, CORNERS)
+    each(five_copy, 1, sends_to, start)
 
     @pl.when((swap(r % 4) == r % 4) & (swap(c % 4) == c % 4))
     def _():

time: 40.3 us -> 38.4 us (0.953)
  the two profiles are of different devices: /device:TPU:1 before, /device:TPU:80 now
where the time goes in v3:
time: 38.4 us; the launch traced here: 38.2 us
  Pallas kernels  36.5 us (95%)
  local copies, waits for them, and re-layouts  1.77 us (5%)
    pallas_call x1, Pallas kernels, local(): pl.pallas_call(kernel, out_shape=jax.ShapeDtypeStruct((4, 4, 48, C), F32)...  36.5 us
    unnamed x1, local copies, waits for them, and re-layouts  1.77 us

profile of v3, /device:TPU:80, one launch (start us, length us, event | category | flops | bytes accessed | tf_op | source)
XLA Modules:
  0.0 38.2 jit_solution(9205270183633254275)
XLA Ops:
  0.0 36.5 %shard_map.55 = f32[4,4,48,121]{3,2,1,0:T(8,128)} custom-call(f32[4,4,48,121]{3,2,1,0:T(8,128)} %bitcast.9, s32[4,4,48]{2,1,0:T(4,128)} %occ.1, bf16[968,121]{1,0:T(8,128)(2,1)} %bitcast.10, bf16[968,121]{1,0:T(8,128)(2,1)} %bitcast.11, bf16[7,7,7,121,121]{4,3,2,1,0:T(8,128)(2,1)} %ops_hbm.1), custom_call_target="tpu_custom_call" | custom-call | tf_op jit(solution)/shard_map/pallas_call | solution.py:531
  36.5 1.8 %copy.7 = f32[121,4,4,48]{0,3,2,1:T(8,128)} copy(f32[121,4,4,48]{0,3,2,1:T(8,128)} %bitcast.8) | data formatting | bytes 743424
